TPU v7x, 32 devices: a whole 2x2x4 slice. The times are simulated.
32 devices in a mesh: groups: 2 (over x), gr: 16 (over z, y, core).
Axes of the slice: x: 2, y: 2, z: 4, core: 2. Of those that a mesh axis runs over, the one named last changes fastest.
Arguments:
- embeddings: bfloat16 [131072, 768], P(('groups', 'gr')), parts along dimension 0
- coverage: bfloat16 [131072], P(('groups', 'gr')), parts along dimension 0, may hold values from 0 to 0.5
- cluster: int32 [131072, 1], P(('groups', 'gr')), parts along dimension 0, may hold values from 0 to 31; in each aligned block of 4096 rows (0 to 4095, 4096 to 8191, ...) at most 192 rows name the same one
- candidates: int32 [64, 1024], P(('groups', 'gr')), parts along dimension 0, may hold values from 0 to 3071
Outputs:
- cluster_gains: float32 [64, 1024], P(('groups', 'gr')), parts along dimension 0
- new_coverage: float32 [131072], P(('groups', 'gr')), parts along dimension 0
There are 2 independent parts, one for each index of `groups`. A program takes and returns all parts, laid end to end along the dimension named above; each array names one. Nothing has to cross between parts.
Inputs may be any that keep to these rules, and one draw needn't show every extreme that they name: Every one of the 32 clusters is named by at least one row. Among the 4096 rows of one device (aligned blocks) no cluster is named more than 192 times, a bound that some block reaches.
All inputs are finite; a program needn't handle non-finite values.
Results may differ from a plain program's by a relative error of at most 0.0006.
Values may be sent and summed in bfloat16 or wider, within the bound.
A program may use at most 128 MiB of HBM per device.

v0:
```python
import jax
import jax.numpy as jnp
from jax import lax
from jax.sharding import PartitionSpec as P


def unit_rows(embeddings):
    widened = embeddings.astype(jnp.float32)
    inverse = lax.rsqrt(jnp.sum(widened * widened, axis=1, keepdims=True) + 1e-06)
    return (widened * inverse).astype(jnp.bfloat16)


def place_of(picked_rank, running, offsets, capacity):
    source = jnp.sum(
        (running[None, :] <= picked_rank[:, None]).astype(jnp.int32), axis=1, dtype=jnp.int32
    )
    matches = jnp.arange(running.shape[0], dtype=jnp.int32)[None, :] == source[:, None]
    offset = picked_rank - jnp.sum(jnp.where(matches, offsets[None, :], 0), axis=1, dtype=jnp.int32)
    return source * capacity + offset


def score_cluster(item_rows, item_cover, item_counts, raw_rank, average):
    sources, capacity, feature_count = item_rows.shape
    slot_count = sources * capacity
    flat_rows = item_rows.reshape(slot_count, feature_count)
    flat_cover = item_cover.reshape(slot_count).astype(jnp.float32)
    running = jnp.cumsum(item_counts)
    offsets = running - item_counts
    headcount = running[-1]
    picked_rank = raw_rank % headcount
    chosen = jnp.take(flat_rows, place_of(picked_rank, running, offsets, capacity), axis=0)
    cand_count = chosen.shape[0]
    block_rows = min(512, cand_count)
    is_live = (jnp.arange(capacity, dtype=jnp.int32)[None, :] < item_counts[:, None]).reshape(
        slot_count
    )

    def one_block(cand_panel):
        scores = jnp.einsum("cd,sd->cs", cand_panel, flat_rows, preferred_element_type=jnp.float32)
        relief = jnp.where(is_live[None, :], jnp.maximum(scores - flat_cover[None, :], 0.0), 0.0)
        return (jnp.sum(relief, axis=1) / average, jnp.max(scores, axis=0))

    gained, nearest = lax.map(
        one_block, chosen.reshape(cand_count // block_rows, block_rows, feature_count)
    )
    return (gained.reshape(cand_count), jnp.max(nearest, axis=0))


def score_items(pieces, candidates, average):
    got_rows, got_cover, got_counts, got_ids = pieces
    item_count = got_rows.shape[1]
    capacity = got_rows.shape[2]

    def one_item(item_no):
        item_rows = lax.dynamic_index_in_dim(got_rows, item_no, 1, keepdims=False)
        item_cover = lax.dynamic_index_in_dim(got_cover, item_no, 1, keepdims=False)
        item_counts = lax.dynamic_index_in_dim(got_counts, item_no, 1, keepdims=False)
        local_slot = lax.dynamic_index_in_dim(got_ids, item_no, 1, keepdims=False)[0]
        raw_rank = lax.dynamic_index_in_dim(candidates, local_slot, 0, keepdims=False)
        return score_cluster(item_rows, item_cover, item_counts, raw_rank, average)

    gained, nearest = lax.map(one_item, jnp.arange(item_count, dtype=jnp.int32))
    return (gained.T, jnp.transpose(nearest.reshape(item_count, -1, capacity), (1, 0, 2)))


def on_device(embeddings, coverage, cluster, candidates):
    owners = lax.axis_size("gr")
    owned_count = candidates.shape[0]
    local_rows = embeddings.shape[0]
    average = local_rows // owned_count
    capacity = 3 * local_rows // (2 * owned_count * owners)
    cluster_total = owned_count * owners
    slot_total = cluster_total * capacity
    normed = unit_rows(embeddings)
    feature_count = normed.shape[1]
    labels = cluster[:, 0]
    onehot = (labels[:, None] == jnp.arange(cluster_total, dtype=jnp.int32)[None, :]).astype(
        jnp.int32
    )
    before = jnp.cumsum(onehot, axis=0) - onehot
    within = jnp.sum(before * onehot, axis=1, dtype=jnp.int32)
    target = labels * capacity + within
    send_rows = (
        jnp.zeros((slot_total, feature_count), jnp.bfloat16)
        .at[target]
        .set(normed)
        .reshape(owners, owned_count, capacity, feature_count)
    )
    send_cover = (
        jnp.zeros((slot_total,), jnp.bfloat16)
        .at[target]
        .set(coverage)
        .reshape(owners, owned_count, capacity)
    )
    counts = jnp.sum(onehot, axis=0, dtype=jnp.int32).reshape(owners, owned_count)
    slot_ids = jnp.broadcast_to(
        jnp.arange(owned_count, dtype=jnp.int32)[None, :], (owners, owned_count)
    )
    pieces = (
        lax.all_to_all(send_rows, "gr", split_axis=0, concat_axis=0, tiled=True),
        lax.all_to_all(send_cover, "gr", split_axis=0, concat_axis=0, tiled=True),
        lax.all_to_all(counts, "gr", split_axis=0, concat_axis=0, tiled=True),
        lax.all_to_all(slot_ids, "gr", split_axis=0, concat_axis=0, tiled=True),
    )
    gain_table, nearest = score_items(pieces, candidates, average)
    returned = lax.all_to_all(nearest, "gr", split_axis=0, concat_axis=0, tiled=True)
    own_nearest = jnp.take(returned.reshape(slot_total), target)
    new_coverage = jnp.maximum(coverage.astype(jnp.float32), own_nearest)
    return (gain_table.T, new_coverage)


def solution(mesh):
    placed = (
        P(("groups", "gr"), None),
        P(("groups", "gr")),
        P(("groups", "gr"), None),
        P(("groups", "gr"), None),
    )
    return jax.shard_map(
        on_device,
        mesh=mesh,
        in_specs=placed,
        out_specs=(P(("groups", "gr"), None), P(("groups", "gr"))),
        check_vma=False,
    )
```

profile of v0, /device:TPU:0, one launch (start us, length us, event | category | flops | bytes accessed | tf_op | source)
XLA Modules:
  0.0 403.3 jit_solution(1686722608313520179)
XLA Ops:
  1.5 9.2 %reduce-window.10 = s32[32,32,128]{2,1,0:T(8,128)S(1)} reduce-window(s32[32,32,128]{2,1,0:T(8,128)S(1)} %fusion.17, s32[]{:T(128)} %constant.104.clone.1), window={size=1x1x128 pad=0_0x0_0x127_0}, to_apply=%region_0.0 | reduce-window | flops 16646144 | bytes 1048580 | tf_op jit(solution)/shard_map/reduce-window.1
  13.9 7.4 %all-to-all-start = ((s32[16,1,2]{2,1,0:T(1,128)}), s32[16,1,2]{2,1,0:T(1,128)S(1)}, u32[]{:S(2)}, u32[]{:S(2)}) async-start(s32[16,1,2]{2,1,0:T(1,128)} %bitcast.13), calls=%async_computation | async-start | bytes 16384 | tf_op jit(solution)/shard_map/all_to_all | solution.py:102
  21.3 4.1 %fusion.9 = f32[4096]{0:T(1024)S(1)} fusion(bf16[4096,768]{1,0:T(8,128)(2,1)} %param.8), kind=kLoop, calls=%fused_computation.35 | loop fusion | flops 9433088 | bytes 6307840 | tf_op jit(solution)/shard_map/reduce_sum | solution.py:9
  26.1 1.5 all-to-all-done
  28.2 4.5 %all-to-all-start.1 = ((s32[16,1,2]{2,1,0:T(1,128)}), s32[16,1,2]{2,1,0:T(1,128)S(1)}, u32[]{:S(2)}, u32[]{:S(2)}) async-start(s32[16,1,2]{2,1,0:T(1,128)} %broadcast_in_dim.81), calls=%async_computation.1 | async-start | bytes 16384 | tf_op jit(solution)/shard_map/all_to_all | solution.py:103
  32.7 28.7 %scatter_custom_fusion.1 = bf16[6144]{0:T(1024)(128)(2,1)S(1)} fusion(s32[4096]{0:T(1024)S(1)} %bitcast.110, bf16[4096]{0:T(1024)(128)(2,1)} %param.9, bf16[]{:T(256)} %constant.106.clone.1), kind=kCustom, calls=%fused_computation.56 | custom fusion | bytes 12800 | tf_op jit(solution)/shard_map/scatter | solution.py:92
  62.1 6.0 %all-to-all-start.3 = ((bf16[16,2,192]{2,1,0:T(2,128)(2,1)}), bf16[16,2,192]{2,1,0:T(2,128)(2,1)S(1)}, u32[]{:S(2)}, u32[]{:S(2)}) async-start(bf16[16,2,192]{2,1,0:T(2,128)(2,1)} %reshape.179), calls=%async_computation.3 | async-start | bytes 32768 | tf_op jit(solution)/shard_map/all_to_all | solution.py:101
  68.2 25.8 %scatter_custom_fusion = bf16[6144,768]{1,0:T(8,128)(2,1)} fusion(s32[4096]{0:T(1024)S(1)} %bitcast.111, bf16[4096,768]{1,0:T(8,128)(2,1)} %param.8, f32[4096]{0:T(1024)S(1)} %add_rsqrt_fusion, bf16[]{:T(256)} %constant.106.clone.1), kind=kCustom, calls=%fused_computation.37 | custom fusion | flops 9437184 | bytes 15745026 | tf_op jit(solution)/shard_map/scatter | solution.py:86
  94.0 6.2 %all-to-all-start.2 = ((bf16[16,2,192,768]{3,2,1,0:T(8,128)(2,1)}), bf16[16,2,192,768]{3,2,1,0:T(8,128)(2,1)}, u32[]{:S(2)}, u32[]{:S(2)}) async-start(bf16[16,2,192,768]{3,2,1,0:T(8,128)(2,1)} %bitcast.94), calls=%async_computation.2 | async-start | bytes 18874368 | tf_op jit(solution)/shard_map/all_to_all | solution.py:100
  100.4 168.8 %all-to-all-done.2 = bf16[16,2,192,768]{3,2,1,0:T(8,128)(2,1)} async-done(((bf16[16,2,192,768]{3,2,1,0:T(8,128)(2,1)}), bf16[16,2,192,768]{3,2,1,0:T(8,128)(2,1)}, u32[]{:S(2)}, u32[]{:S(2)}) %all-to-all-start.2) | async-done | bytes 9437216 | tf_op jit(solution)/shard_map/all_to_all | solution.py:100
  269.2 62.3 %while.26 = (s32[]{:T(128)}, f32[2,1024]{1,0:T(2,128)S(1)}, f32[2,3072]{1,0:T(2,128)S(1)}, s32[2]{0:T(128)S(1)}, s32[16,2]{0,1:T(2,128)S(1)}, /*index=5*/s32[16,...) while((s32[]{:T(128)}, f32[2,1024]{1,0:T(2,128)S(1)}, ...), condition=%wide.region_16.17_spmd, body=%wide.region_7.16_spmd.sunk | while | flops 2424707328 | bytes 21540352 | solution.py:62
  275.7 5.0 %constant_dynamic-slice_fusion.5 = bf16[16,1,192,768]{3,2,1,0:T(8,128)(2,1)} fusion(bf16[16,2,192,768]{3,2,1,0:T(8,128)(2,1)} %get-tuple-element.369, s32[]{:T(128)S(6)} %select_n.125), kind=kLoop, calls=%fused_computation.29.clone.1 | loop fusion | bytes 9437188 | tf_op jit(solution)/shard_map/while/body/eval_jaxpr/jit(dynamic_index_in_dim)/dynamic_slice | solution.py:55
  280.7 7.4 %gather_fusion = bf16[1024,768]{1,0:T(8,128)(2,1)S(1)} fusion(bf16[3072,768]{1,0:T(8,128)(2,1)} %bitcast.91, s32[1024]{0:T(1024)S(1)} %broadcast_clamp_fusion.3), kind=kCustom, calls=%fused_computation.clone.1 | custom fusion | bytes 3149824 | tf_op jit(solution)/shard_map/while/body/eval_jaxpr/jit(_take)/gather | solution.py:31
  288.5 11.5 %while.27 = (s32[]{:T(128)}, f32[2,512]{1,0:T(2,128)S(1)}, f32[2,3072]{1,0:T(2,128)S(1)}, bf16[2,512,768]{2,1,0:T(8,128)(2,1)S(1)}, bf16[3072,768]{1,0:T(8,128)(...) while((s32[]{:T(128)}, f32[2,512]{1,0:T(2,128)S(1)}, ...), condition=%wide.region_14.14_spmd.clone, body=%wide.region_11.13_spmd.clone.sunk | while | flops 2423783424 | bytes 5576873 | solution.py:43
  288.7 5.4 %fusion.28 = (f32[3072]{0:T(1024)S(1)}, f32[512]{0:T(512)S(1)}) fusion(f32[3072]{0:T(1024)S(1)} %get-tuple-element.328, pred[3072]{0:T(1024)(128)(4,1)S(1)} %broadcast_in_dim.107, bf16[3072,768]{1,0:T(8,128)(2,1)} %get-tuple-element.327, bf16[2,512,768]{2,1,0:T(8,128)(2,1)S(1)} %get-tuple-element.326, s32[]{:T(128)} %get-tuple-element.314), kind=kOutput, calls=%fused_computation.58.clone.1 | convolution fusion | flops 2423779840 | bytes 5534724 | tf_op jit(solution)/shard_map/while/body/eval_jaxpr/while/body/eval_jaxpr/cd,sd->cs/dot_general | solution.py:39
  294.4 5.4 %fusion.28 = (f32[3072]{0:T(1024)S(1)}, f32[512]{0:T(512)S(1)}) fusion(f32[3072]{0:T(1024)S(1)} %get-tuple-element.328, pred[3072]{0:T(1024)(128)(4,1)S(1)} %broadcast_in_dim.107, bf16[3072,768]{1,0:T(8,128)(2,1)} %get-tuple-element.327, bf16[2,512,768]{2,1,0:T(8,128)(2,1)S(1)} %get-tuple-element.326, s32[]{:T(128)} %get-tuple-element.314), kind=kOutput, calls=%fused_computation.58.clone.1 | convolution fusion | flops 2423779840 | bytes 5534724 | tf_op jit(solution)/shard_map/while/body/eval_jaxpr/while/body/eval_jaxpr/cd,sd->cs/dot_general | solution.py:39
  306.8 5.0 %constant_dynamic-slice_fusion.5 = bf16[16,1,192,768]{3,2,1,0:T(8,128)(2,1)} fusion(bf16[16,2,192,768]{3,2,1,0:T(8,128)(2,1)} %get-tuple-element.369, s32[]{:T(128)S(6)} %select_n.125), kind=kLoop, calls=%fused_computation.29.clone.1 | loop fusion | bytes 9437188 | tf_op jit(solution)/shard_map/while/body/eval_jaxpr/jit(dynamic_index_in_dim)/dynamic_slice | solution.py:55
  311.8 7.4 %gather_fusion = bf16[1024,768]{1,0:T(8,128)(2,1)S(1)} fusion(bf16[3072,768]{1,0:T(8,128)(2,1)} %bitcast.91, s32[1024]{0:T(1024)S(1)} %broadcast_clamp_fusion.3), kind=kCustom, calls=%fused_computation.clone.1 | custom fusion | bytes 3149824 | tf_op jit(solution)/shard_map/while/body/eval_jaxpr/jit(_take)/gather | solution.py:31
  319.6 11.5 %while.27 = (s32[]{:T(128)}, f32[2,512]{1,0:T(2,128)S(1)}, f32[2,3072]{1,0:T(2,128)S(1)}, bf16[2,512,768]{2,1,0:T(8,128)(2,1)S(1)}, bf16[3072,768]{1,0:T(8,128)(...) while((s32[]{:T(128)}, f32[2,512]{1,0:T(2,128)S(1)}, ...), condition=%wide.region_14.14_spmd.clone, body=%wide.region_11.13_spmd.clone.sunk | while | flops 2423783424 | bytes 5576873 | solution.py:43
  319.8 5.4 %fusion.28 = (f32[3072]{0:T(1024)S(1)}, f32[512]{0:T(512)S(1)}) fusion(f32[3072]{0:T(1024)S(1)} %get-tuple-element.328, pred[3072]{0:T(1024)(128)(4,1)S(1)} %broadcast_in_dim.107, bf16[3072,768]{1,0:T(8,128)(2,1)} %get-tuple-element.327, bf16[2,512,768]{2,1,0:T(8,128)(2,1)S(1)} %get-tuple-element.326, s32[]{:T(128)} %get-tuple-element.314), kind=kOutput, calls=%fused_computation.58.clone.1 | convolution fusion | flops 2423779840 | bytes 5534724 | tf_op jit(solution)/shard_map/while/body/eval_jaxpr/while/body/eval_jaxpr/cd,sd->cs/dot_general | solution.py:39
  325.6 5.4 %fusion.28 = (f32[3072]{0:T(1024)S(1)}, f32[512]{0:T(512)S(1)}) fusion(f32[3072]{0:T(1024)S(1)} %get-tuple-element.328, pred[3072]{0:T(1024)(128)(4,1)S(1)} %broadcast_in_dim.107, bf16[3072,768]{1,0:T(8,128)(2,1)} %get-tuple-element.327, bf16[2,512,768]{2,1,0:T(8,128)(2,1)S(1)} %get-tuple-element.326, s32[]{:T(128)} %get-tuple-element.314), kind=kOutput, calls=%fused_computation.58.clone.1 | convolution fusion | flops 2423779840 | bytes 5534724 | tf_op jit(solution)/shard_map/while/body/eval_jaxpr/while/body/eval_jaxpr/cd,sd->cs/dot_general | solution.py:39
  332.2 40.7 %all-to-all-start.4 = ((f32[16,2,192]{2,1,0:T(2,128)}), f32[16,2,192]{2,1,0:T(2,128)S(1)}, u32[]{:S(2)}, u32[]{:S(2)}) async-start(f32[16,2,192]{2,1,0:T(2,128)} %bitcast.48), calls=%async_computation.4 | async-start | bytes 65536 | tf_op jit(solution)/shard_map/all_to_all | solution.py:106
  372.9 6.6 %all-to-all-done.4 = f32[16,2,192]{2,1,0:T(2,128)S(1)} async-done(((f32[16,2,192]{2,1,0:T(2,128)}), f32[16,2,192]{2,1,0:T(2,128)S(1)}, u32[]{:S(2)}, u32[]{:S(2)}) %all-to-all-start.4) | async-done | bytes 24608 | tf_op jit(solution)/shard_map/all_to_all | solution.py:106
  379.6 23.0 %gather_fusion.1 = f32[4096]{0:T(1024)S(1)} fusion(f32[6144]{0:T(1024)S(1)} %reshape.181, s32[4096]{0:T(1024)S(1)} %broadcast_clamp_fusion.1), kind=kCustom, calls=%fused_computation.1 | custom fusion | bytes 49152 | tf_op jit(solution)/shard_map/jit(_take)/gather | solution.py:107
  (112 shorter events, 16.3 us)
Async XLA Ops:
  0.6 24.7 %copy-start = (s32[4096,1]{0,1:T(1,128)S(1)}, s32[4096,1]{0,1:T(1,128)}, u32[]{:S(2)}) copy-start(s32[4096,1]{0,1:T(1,128)} %param.10) | copy-start | bytes 49156
  13.9 13.7 %all-to-all-start = ((s32[16,1,2]{2,1,0:T(1,128)}), s32[16,1,2]{2,1,0:T(1,128)S(1)}, u32[]{:S(2)}, u32[]{:S(2)}) async-start(s32[16,1,2]{2,1,0:T(1,128)} %bitcast.13), calls=%async_computation | async-start | bytes 16384 | tf_op jit(solution)/shard_map/all_to_all | solution.py:102
  26.0 67.9 %copy-start.1 = (s32[4096,1]{0,1:T(1,128)}, s32[4096,1]{0,1:T(1,128)S(1)}, u32[]{:S(2)}) copy-start(s32[4096,1]{0,1:T(1,128)S(1)} %get-tuple-element.173) | copy-start | bytes 49156
  28.2 33.9 %all-to-all-start.1 = ((s32[16,1,2]{2,1,0:T(1,128)}), s32[16,1,2]{2,1,0:T(1,128)S(1)}, u32[]{:S(2)}, u32[]{:S(2)}) async-start(s32[16,1,2]{2,1,0:T(1,128)} %broadcast_in_dim.81), calls=%async_computation.1 | async-start | bytes 16384 | tf_op jit(solution)/shard_map/all_to_all | solution.py:103
  62.1 31.9 %all-to-all-start.3 = ((bf16[16,2,192]{2,1,0:T(2,128)(2,1)}), bf16[16,2,192]{2,1,0:T(2,128)(2,1)S(1)}, u32[]{:S(2)}, u32[]{:S(2)}) async-start(bf16[16,2,192]{2,1,0:T(2,128)(2,1)} %reshape.179), calls=%async_computation.3 | async-start | bytes 32768 | tf_op jit(solution)/shard_map/all_to_all | solution.py:101
  94.0 175.2 %copy-start.3 = (s32[2,1024]{1,0:T(2,128)S(1)}, s32[2,1024]{1,0:T(2,128)}, u32[]{:S(2)}) copy-start(s32[2,1024]{1,0:T(2,128)} %param.11) | copy-start | bytes 24580
  94.0 175.2 %all-to-all-start.2 = ((bf16[16,2,192,768]{3,2,1,0:T(8,128)(2,1)}), bf16[16,2,192,768]{3,2,1,0:T(8,128)(2,1)}, u32[]{:S(2)}, u32[]{:S(2)}) async-start(bf16[16,2,192,768]{3,2,1,0:T(8,128)(2,1)} %bitcast.94), calls=%async_computation.2 | async-start | bytes 18874368 | tf_op jit(solution)/shard_map/all_to_all | solution.py:100
  269.2 103.7 %copy-start.2 = (s32[4096,1]{0,1:T(1,128)S(1)}, s32[4096,1]{0,1:T(1,128)}, u32[]{:S(2)}) copy-start(s32[4096,1]{0,1:T(1,128)} %copy-done.1) | copy-start | bytes 49156
  331.4 71.2 %copy-start.6 = (f32[2,1024]{1,0:T(2,128)}, f32[2,1024]{1,0:T(2,128)S(1)}, u32[]{:S(2)}) copy-start(f32[2,1024]{1,0:T(2,128)S(1)} %get-tuple-element.86) | copy-start | bytes 24580
  332.2 47.4 %all-to-all-start.4 = ((f32[16,2,192]{2,1,0:T(2,128)}), f32[16,2,192]{2,1,0:T(2,128)S(1)}, u32[]{:S(2)}, u32[]{:S(2)}) async-start(f32[16,2,192]{2,1,0:T(2,128)} %bitcast.48), calls=%async_computation.4 | async-start | bytes 65536 | tf_op jit(solution)/shard_map/all_to_all | solution.py:106
  379.6 23.1 %copy-start.4 = (pred[4096]{0:T(1024)(128)(4,1)S(1)}, pred[4096]{0:T(1024)(128)(4,1)}, u32[]{:S(2)}) copy-start(pred[4096]{0:T(1024)(128)(4,1)} %get-tuple-element.172) | copy-start | bytes 12292
  379.6 23.1 %copy-start.5 = (bf16[4096]{0:T(1024)(128)(2,1)S(1)}, bf16[4096]{0:T(1024)(128)(2,1)}, u32[]{:S(2)}) copy-start(bf16[4096]{0:T(1024)(128)(2,1)} %param.9) | copy-start | bytes 24580
where the time goes:
time: 404 us; the launch traced here: 403 us
  waiting for transfers between devices  177 us (44%)
  local copies, waits for them, and re-layouts  85.4 us (21%)
  starting transfers between devices  64.8 us (16%)
  other arithmetic  46.7 us (12%)
  matrix products  21.6 us (5%)
  loops' own time  7.09 us (2%)
    all_to_all x1, waiting for transfers between devices, on_device(): lax.all_to_all(send_rows, 'gr', split_axis=0, concat_axis=0, tiled=True)  169 us
    all_to_all x1, starting transfers between devices, on_device(): lax.all_to_all(nearest, 'gr', split_axis=0, concat_axis=0, tiled=True)  40.7 us
    scatter x1, local copies, waits for them, and re-layouts, on_device(): send_cover = jnp.zeros((slot_total,), jnp.bfloat16).at[target].set(covera...  28.7 us
    scatter x1, other arithmetic, on_device(): send_rows = jnp.zeros((slot_total, feature_count), jnp.bfloat16).at[targe...  25.8 us
    gather x1, local copies, waits for them, and re-layouts, on_device(): own_nearest = jnp.take(returned.reshape(slot_total), target)  23 us
    dot_general x4, matrix products, one_block(): jnp.einsum('cd,sd->cs', cand_panel, flat_rows, preferred_element_type=jnp...  21.6 us
    gather x2, local copies, waits for them, and re-layouts, score_cluster(): jnp.take(flat_rows, place_of(picked_rank, running, offsets, capacity), ax...  14.8 us
    dynamic_slice x2, local copies, waits for them, and re-layouts, one_item(): item_rows = lax.dynamic_index_in_dim(got_rows, item_no, 1, keepdims=False)  10 us
  transfers between devices with their start and end apart: 5, of which 3 were waited for; matrix products, arithmetic and copies ran while one was open for 15% of the time, Pallas kernels for 0%

commit v1 on v0

v1 whole, which is shorter than its diff:
```python
import functools
import jax
import jax.numpy as jnp
from jax import lax
from jax.experimental import pallas as pl
from jax.experimental.pallas import tpu as pltpu
from jax.sharding import PartitionSpec as P

DEAD = 4.0
F32 = jnp.float32
BF16 = jnp.bfloat16


def unit_rows(embeddings):
    widened = embeddings.astype(F32)
    inverse = lax.rsqrt(jnp.sum(widened * widened, axis=1, keepdims=True) + 1e-06)
    return (widened * inverse).astype(BF16)


def kernel(
    n, owned, cap, average,
    normed, labels, cover, raw,
    gains, fresh,
    target, send, got, send_aux, got_aux, chosen_sum, chosen, relief_sum, near_out, near_in, near_all,
    row_sent, row_here, aux_sent, aux_here, near_sent, near_here,
):
    me = lax.axis_index("gr")
    half = n // 2
    rows = normed.shape[0]
    cands = raw.shape[1]
    clusters = n * owned

    def partner(step):
        same = step // half
        block = (1 - me // half) * (1 - same) + (me // half) * same
        return block * half + (me % half + step % half + same) % half

    barrier = pltpu.get_barrier_semaphore()

    def greet(step, carry):
        pl.semaphore_signal(barrier, inc=1, device_id={"gr": partner(step)}, device_id_type=pl.DeviceIdType.MESH)
        return carry

    lax.fori_loop(0, n - 1, greet, 0)

    tile = 256
    upper = (
        lax.broadcasted_iota(jnp.int32, (tile, tile), 0) < lax.broadcasted_iota(jnp.int32, (tile, tile), 1)
    ).astype(F32).astype(BF16)
    running = jnp.zeros((clusters, 1), F32)
    for block in range(rows // tile):
        span = slice(block * tile, (block + 1) * tile)
        label = labels[:, span]
        hot = (lax.broadcasted_iota(jnp.int32, (clusters, tile), 0) == label).astype(F32)
        before = jnp.dot(hot.astype(BF16), upper, preferred_element_type=F32) + running
        running = running + jnp.sum(hot, axis=1, keepdims=True)
        within = jnp.sum(before * hot, axis=0, keepdims=True)
        target[:, span] = label * cap + within.astype(jnp.int32)

    pl.semaphore_wait(barrier, n - 1)

    def packed(owner, item):
        base = (owner * owned + item) * cap
        hot = (
            lax.broadcasted_iota(jnp.int32, (cap, rows), 0) + base == target[...]
        ).astype(F32).astype(BF16)
        block = jnp.dot(hot, normed[...], preferred_element_type=F32).astype(BF16)
        pair = lax.dot_general(cover[...], hot, (((1,), (1,)), ((), ())), preferred_element_type=F32)
        return block, pair[0:1, :] + DEAD * (1.0 - pair[1:2, :])

    def row_copy(owner, item):
        return pltpu.make_async_remote_copy(
            src_ref=send.at[item, owner], dst_ref=got.at[item, me],
            send_sem=row_sent.at[item, owner], recv_sem=row_here.at[item, me],
            device_id={"gr": owner}, device_id_type=pl.DeviceIdType.MESH,
        )

    def aux_copy(owner, item):
        return pltpu.make_async_remote_copy(
            src_ref=send_aux.at[item, owner], dst_ref=got_aux.at[item, me],
            send_sem=aux_sent.at[item, owner], recv_sem=aux_here.at[item, me],
            device_id={"gr": owner}, device_id_type=pl.DeviceIdType.MESH,
        )

    def near_copy(source, item):
        return pltpu.make_async_remote_copy(
            src_ref=near_out.at[item, source], dst_ref=near_in.at[item, me],
            send_sem=near_sent.at[item, source], recv_sem=near_here.at[item, me],
            device_id={"gr": source}, device_id_type=pl.DeviceIdType.MESH,
        )

    def arrived(ref, sem, source, item):
        pltpu.make_async_remote_copy(
            src_ref=ref.at[item, source], dst_ref=ref.at[item, source],
            send_sem=sem.at[item, source], recv_sem=sem.at[item, source],
            device_id={"gr": source}, device_id_type=pl.DeviceIdType.MESH,
        ).wait_recv()

    def send_item(item, carry):
        def send_one(step, carry):
            owner = partner(step)
            block, aux = packed(owner, item)
            send_aux[item, owner] = aux
            aux_copy(owner, item).start()
            send[item, owner] = block
            row_copy(owner, item).start()
            return carry

        lax.fori_loop(0, n - 1, send_one, 0)
        block, aux = packed(me, item)
        got_aux[item, me] = aux
        got[item, me] = block
        return carry

    lax.fori_loop(0, owned, send_item, 0)

    def score_item(item, carry):
        def await_one(step, carry):
            source = partner(step)
            arrived(got_aux, aux_here, source, item)
            arrived(got, row_here, source, item)
            return carry

        lax.fori_loop(0, n - 1, await_one, 0)

        def count_one(source, total):
            return total + jnp.sum((got_aux[item, source] < 2.0).astype(F32), axis=1, keepdims=True)

        total = lax.fori_loop(0, n, count_one, jnp.zeros((1, 1), F32))
        ranks = raw[item]
        picked = ranks - jnp.floor(ranks / total) * total
        picked = jnp.where(picked < 0.0, picked + total, picked)
        picked = jnp.where(picked >= total, picked - total, picked)
        chosen_sum[...] = jnp.zeros_like(chosen_sum)

        def gather_one(source, start):
            live = got_aux[item, source] < 2.0
            place = lax.broadcasted_iota(jnp.int32, (1, cap), 1).astype(F32) + start
            place = jnp.where(live, place, -1.0)
            hot = (place == picked).astype(F32).astype(BF16)
            chosen_sum[...] += jnp.dot(hot, got[item, source], preferred_element_type=F32)
            return start + jnp.sum(live.astype(F32), axis=1, keepdims=True)

        lax.fori_loop(0, n, gather_one, jnp.zeros((1, 1), F32))
        chosen[...] = chosen_sum[...].astype(BF16)
        relief_sum[...] = jnp.zeros_like(relief_sum)

        def score_one(source, carry):
            scores = lax.dot_general(
                chosen[...], got[item, source], (((1,), (1,)), ((), ())), preferred_element_type=F32
            )
            relief_sum[...] += jnp.maximum(scores - got_aux[item, source], 0.0)
            near_out[item, source] = jnp.max(scores, axis=0, keepdims=True)
            return carry

        lax.fori_loop(0, n, score_one, 0)

        def send_back(step, carry):
            near_copy(partner(step), item).start()
            return carry

        lax.fori_loop(0, n - 1, send_back, 0)
        near_in[item, me] = near_out[item, me]
        gains[item] = jnp.sum(relief_sum[...], axis=1, keepdims=True) / average
        return carry

    lax.fori_loop(0, owned, score_item, 0)

    def finish(step, carry):
        other = partner(step)
        for item in range(owned):
            row_copy(other, item).wait_send()
            aux_copy(other, item).wait_send()
            near_copy(other, item).wait_send()
            arrived(near_in, near_here, other, item)
        return carry

    lax.fori_loop(0, n - 1, finish, 0)

    for owner in range(n):
        for item in range(owned):
            k = owner * owned + item
            near_all[k : k + 1, :] = near_in[item, owner]
    table = near_all[...]
    first = table.astype(BF16)
    rest = table - first.astype(F32)
    second = rest.astype(BF16)
    third = (rest - second.astype(F32)).astype(BF16)
    parts = [part.astype(F32).T.astype(BF16) for part in (first, second, third)]
    for block in range(rows // 512):
        span = slice(block * 512, (block + 1) * 512)
        label = labels[:, span]
        hot = (lax.broadcasted_iota(jnp.int32, (clusters, 512), 0) == label).astype(F32).astype(BF16)
        columns = sum(jnp.dot(part, hot, preferred_element_type=F32) for part in parts)
        slot = target[:, span] - label * cap
        match = lax.broadcasted_iota(jnp.int32, (cap, 512), 0) == slot
        value = jnp.sum(jnp.where(match, columns, 0.0), axis=0, keepdims=True)
        fresh[:, span] = jnp.maximum(cover[0:1, span].astype(F32), value)


def on_device(embeddings, coverage, cluster, candidates):
    n = lax.axis_size("gr")
    owned, cands = candidates.shape
    rows, width = embeddings.shape
    average = rows // owned
    cap = 3 * rows // (2 * owned * n)
    normed = unit_rows(embeddings)
    cover = jnp.concatenate(
        [coverage.reshape(1, rows), jnp.ones((1, rows), BF16), jnp.zeros((14, rows), BF16)], axis=0
    )
    raw = candidates.astype(F32).reshape(owned, cands, 1)
    vmem = pl.BlockSpec(memory_space=pltpu.VMEM)
    dma = pltpu.SemaphoreType.DMA((owned, n))
    gains, fresh = pl.pallas_call(
        functools.partial(kernel, n, owned, cap, average),
        out_shape=(
            jax.ShapeDtypeStruct((owned, cands, 1), F32),
            jax.ShapeDtypeStruct((1, rows), F32),
        ),
        in_specs=[vmem] * 4,
        out_specs=(vmem, vmem),
        scratch_shapes=[
            pltpu.VMEM((1, rows), jnp.int32),
            pltpu.VMEM((owned, n, cap, width), BF16),
            pltpu.VMEM((owned, n, cap, width), BF16),
            pltpu.VMEM((owned, n, 1, cap), F32),
            pltpu.VMEM((owned, n, 1, cap), F32),
            pltpu.VMEM((cands, width), F32),
            pltpu.VMEM((cands, width), BF16),
            pltpu.VMEM((cands, cap), F32),
            pltpu.VMEM((owned, n, 1, cap), F32),
            pltpu.VMEM((owned, n, 1, cap), F32),
            pltpu.VMEM((n * owned, cap), F32),
        ] + [dma] * 6,
        compiler_params=pltpu.CompilerParams(
            collective_id=0, has_side_effects=True, vmem_limit_bytes=60 * 1024 * 1024
        ),
    )(normed, cluster.reshape(1, rows), cover, raw)
    return (gains.reshape(owned, cands), fresh.reshape(rows))


def solution(mesh):
    placed = (
        P(("groups", "gr"), None),
        P(("groups", "gr")),
        P(("groups", "gr"), None),
        P(("groups", "gr"), None),
    )
    return jax.shard_map(
        on_device,
        mesh=mesh,
        in_specs=placed,
        out_specs=(P(("groups", "gr"), None), P(("groups", "gr"))),
        check_vma=False,
    )
```

time: 404 us -> 270 us (0.67)
  Pallas kernels: 0 us -> 250 us
  waiting for transfers between devices: 177 us -> 0 us
  local copies, waits for them, and re-layouts: 85.4 us -> 3.57 us
  starting transfers between devices: 64.8 us -> 0 us
  other arithmetic: 46.7 us -> 15 us
  matrix products: 21.6 us -> 0 us
  loops' own time: 7.09 us -> 0 us
    pallas_call x0 -> x1, Pallas kernels: none -> 250 us  [on_device(): pl.pallas_call(functools.partial(kernel, n, owned, cap, average), out_sha...]
    all_to_all x5 -> x0, waiting for transfers between devices: 177 us -> none  [the longest x1 169 us: on_device(): lax.all_to_all(send_rows, 'gr', split_axis=0, concat_axis=0, tiled=True)]
    all_to_all x5 -> x0, starting transfers between devices: 64.8 us -> none  [the longest x1 40.7 us: on_device(): lax.all_to_all(nearest, 'gr', split_axis=0, concat_axis=0, tiled=True)]
    gather x3 -> x0, local copies, waits for them, and re-layouts: 37.9 us -> none  [the longest x1 23 us: on_device(): own_nearest = jnp.take(returned.reshape(slot_total), target)]
    scatter x1 -> x0, local copies, waits for them, and re-layouts: 28.7 us -> none  [on_device(): send_cover = jnp.zeros((slot_total,), jnp.bfloat16).at[target].set(covera...]
    scatter x1 -> x0, other arithmetic: 25.8 us -> none  [on_device(): send_rows = jnp.zeros((slot_total, feature_count), jnp.bfloat16).at[targe...]
    dot_general x4 -> x0, matrix products: 21.6 us -> none  [one_block(): jnp.einsum('cd,sd->cs', cand_panel, flat_rows, preferred_element_type=jnp...]
    dynamic_slice x8 -> x0, local copies, waits for them, and re-layouts: 11.4 us -> none  [the longest x2 10 us: one_item(): item_rows = lax.dynamic_index_in_dim(got_rows, item_no, 1, keepdims=False)]
  transfers between devices with their start and end apart: 5 -> 0, of which waited for: 3 -> 0; matrix products, arithmetic and copies ran while one was open for 15% -> 0% of each run, Pallas kernels for 0% -> 0%
where the time goes in v1:
time: 270 us; the launch traced here: 269 us
  Pallas kernels  250 us (93%)
  other arithmetic  15 us (6%)
  local copies, waits for them, and re-layouts  3.57 us (1%)
    pallas_call x1, Pallas kernels, on_device(): pl.pallas_call(functools.partial(kernel, n, owned, cap, average), out_sha...  250 us
    convert_element_type x1, other arithmetic, unit_rows(): return (widened * inverse).astype(BF16)  7.26 us

profile of v1, /device:TPU:0, one launch (start us, length us, event | category | flops | bytes accessed | tf_op | source)
XLA Modules:
  0.0 269.1 jit_solution(13672997996840086908)
XLA Ops:
  0.6 0.1 pad.1.clone
  0.7 0.1 pad.2.clone
  0.8 0.7 convert_bitcast_fusion
  1.5 0.7 reshape.26
  2.2 4.1 %fusion = f32[4096]{0:T(1024)S(1)} fusion(bf16[4096,768]{1,0:T(8,128)(2,1)} %param.4), kind=kLoop, calls=%fused_computation.2 | loop fusion | flops 9433088 | bytes 6307840 | tf_op jit(solution)/shard_map/reduce_sum | solution.py:16
  6.3 0.7 maximum_maximum_fusion.cover
  7.0 1.4 copy.6.raw
  8.4 7.3 %fusion.1.normed = bf16[4096,768]{1,0:T(8,128)(2,1)} fusion(bf16[4096,768]{1,0:T(8,128)(2,1)} %param.4, f32[4096]{0:T(1024)S(1)} %add_rsqrt_fusion), kind=kLoop, calls=%fused_computation.3 | loop fusion | flops 9437184 | bytes 12599296 | tf_op jit(solution)/shard_map/convert_element_type | solution.py:17
  15.7 249.9 %shard_map.59 = (f32[2,1024,1]{2,1,0:T(8,128)}, f32[1,4096]{1,0:T(1,128)}) custom-call(bf16[4096,768]{1,0:T(8,128)(2,1)} %fusion.1.normed, s32[1,4096]{1,0:T(1,128)} %bitcast.5, bf16[16,4096]{1,0:T(8,128)(2,1)} %maximum_maximum_fusion.cover, f32[2,1024,1]{2,1,0:T(8,128)} %copy.6.raw), custom_call_target="tpu_custom_call" | custom-call | tf_op jit(solution)/shard_map/pallas_call | solution.py:214
  265.6 2.2 reduce
  267.8 1.3 copy.8
  (2 shorter events, 0.0 us)

commit v2 on v1

--- a/solution.py
+++ b/solution.py
@@ -11,29 +11,32 @@
 BF16 = jnp.bfloat16
 
 
-def unit_rows(embeddings):
-    widened = embeddings.astype(F32)
-    inverse = lax.rsqrt(jnp.sum(widened * widened, axis=1, keepdims=True) + 1e-06)
-    return (widened * inverse).astype(BF16)
-
-
 def kernel(
     n, owned, cap, average,
-    normed, labels, cover, raw,
+    embeddings, labels, cover, raw,
     gains, fresh,
-    target, send, got, send_aux, got_aux, chosen_sum, chosen, relief_sum, near_out, near_in, near_all,
-    row_sent, row_here, aux_sent, aux_here, near_sent, near_here,
+    held, target, send_count, got_count, starts, send, got, send_aux, got_aux, chosen_sum, chosen, relief_sum, near_out, near_in, near_all,
+    held_in, count_sent, count_here, row_sent, row_here, aux_sent, aux_here, near_sent, near_here,
 ):
     me = lax.axis_index("gr")
     half = n // 2
-    rows = normed.shape[0]
+    rows = held.shape[0]
     cands = raw.shape[1]
     clusters = n * owned
 
+    load = pltpu.make_async_copy(embeddings, held, held_in)
+    load.start()
+
+    def peer(step, sign):
+        turn = 1 - step % 2
+        last = step // (n - 2)
+        across = turn + last - turn * last
+        block = (1 - me // half) * across + (me // half) * (1 - across)
+        shift = step // 2 + 1 - across
+        return block * half + (me % half + half + sign * shift) % half
+
     def partner(step):
-        same = step // half
-        block = (1 - me // half) * (1 - same) + (me // half) * same
-        return block * half + (me % half + step % half + same) % half
+        return peer(step, 1)
 
     barrier = pltpu.get_barrier_semaphore()
 
@@ -57,6 +60,10 @@
         within = jnp.sum(before * hot, axis=0, keepdims=True)
         target[:, span] = label * cap + within.astype(jnp.int32)
 
+    for owner in range(n):
+        send_count[owner] = jnp.broadcast_to(running[owner * owned : (owner + 1) * owned, :], (owned, 128))
+    got_count[me] = send_count[me]
+
     pl.semaphore_wait(barrier, n - 1)
 
     def packed(owner, item):
@@ -64,9 +71,18 @@
         hot = (
             lax.broadcasted_iota(jnp.int32, (cap, rows), 0) + base == target[...]
         ).astype(F32).astype(BF16)
-        block = jnp.dot(hot, normed[...], preferred_element_type=F32).astype(BF16)
+        raised = jnp.dot(hot, held[...], preferred_element_type=F32)
+        inverse = lax.rsqrt(jnp.sum(raised * raised, axis=1, keepdims=True) + 1e-06)
+        block = (raised * inverse).astype(BF16)
         pair = lax.dot_general(cover[...], hot, (((1,), (1,)), ((), ())), preferred_element_type=F32)
         return block, pair[0:1, :] + DEAD * (1.0 - pair[1:2, :])
+
+    def count_copy(owner):
+        return pltpu.make_async_remote_copy(
+            src_ref=send_count.at[owner], dst_ref=got_count.at[me],
+            send_sem=count_sent.at[owner], recv_sem=count_here.at[me],
+            device_id={"gr": owner}, device_id_type=pl.DeviceIdType.MESH,
+        )
 
     def row_copy(owner, item):
         return pltpu.make_async_remote_copy(
@@ -95,6 +111,13 @@
             send_sem=sem.at[item, source], recv_sem=sem.at[item, source],
             device_id={"gr": source}, device_id_type=pl.DeviceIdType.MESH,
         ).wait_recv()
+
+    def send_counts(step, carry):
+        count_copy(partner(step)).start()
+        return carry
+
+    lax.fori_loop(0, n - 1, send_counts, 0)
+    load.wait()
 
     def send_item(item, carry):
         def send_one(step, carry):
@@ -114,34 +137,47 @@
 
     lax.fori_loop(0, owned, send_item, 0)
 
+    def await_counts(step, carry):
+        source = partner(step)
+        pltpu.make_async_remote_copy(
+            src_ref=send_count.at[source], dst_ref=got_count.at[source],
+            send_sem=count_sent.at[source], recv_sem=count_here.at[source],
+            device_id={"gr": source}, device_id_type=pl.DeviceIdType.MESH,
+        ).wait_recv()
+        return carry
+
+    lax.fori_loop(0, n - 1, await_counts, 0)
+    for item in range(owned):
+        ahead = jnp.zeros((1, 128), F32)
+        for source in range(n):
+            starts[item, source] = ahead
+            ahead = ahead + got_count[source][item : item + 1, :]
+        starts[item, n] = ahead
+
     def score_item(item, carry):
-        def await_one(step, carry):
-            source = partner(step)
-            arrived(got_aux, aux_here, source, item)
-            arrived(got, row_here, source, item)
-            return carry
-
-        lax.fori_loop(0, n - 1, await_one, 0)
-
-        def count_one(source, total):
-            return total + jnp.sum((got_aux[item, source] < 2.0).astype(F32), axis=1, keepdims=True)
-
-        total = lax.fori_loop(0, n, count_one, jnp.zeros((1, 1), F32))
+        total = starts[item, n][:, 0:1]
         ranks = raw[item]
         picked = ranks - jnp.floor(ranks / total) * total
         picked = jnp.where(picked < 0.0, picked + total, picked)
         picked = jnp.where(picked >= total, picked - total, picked)
         chosen_sum[...] = jnp.zeros_like(chosen_sum)
 
-        def gather_one(source, start):
-            live = got_aux[item, source] < 2.0
-            place = lax.broadcasted_iota(jnp.int32, (1, cap), 1).astype(F32) + start
-            place = jnp.where(live, place, -1.0)
+        def gather(source):
+            place = lax.broadcasted_iota(jnp.int32, (1, cap), 1).astype(F32) + starts[item, source][:, 0:1]
+            place = jnp.where(got_aux[item, source] < 2.0, place, -1.0)
             hot = (place == picked).astype(F32).astype(BF16)
             chosen_sum[...] += jnp.dot(hot, got[item, source], preferred_element_type=F32)
-            return start + jnp.sum(live.astype(F32), axis=1, keepdims=True)
-
-        lax.fori_loop(0, n, gather_one, jnp.zeros((1, 1), F32))
+
+        gather(me)
+
+        def gather_one(step, carry):
+            source = peer(step, -1)
+            arrived(got_aux, aux_here, source, item)
+            arrived(got, row_here, source, item)
+            gather(source)
+            return carry
+
+        lax.fori_loop(0, n - 1, gather_one, 0)
         chosen[...] = chosen_sum[...].astype(BF16)
         relief_sum[...] = jnp.zeros_like(relief_sum)
 
@@ -161,13 +197,14 @@
 
         lax.fori_loop(0, n - 1, send_back, 0)
         near_in[item, me] = near_out[item, me]
-        gains[item] = jnp.sum(relief_sum[...], axis=1, keepdims=True) / average
+        gains[item] = jnp.sum(relief_sum[...].T, axis=0, keepdims=True) / average
         return carry
 
     lax.fori_loop(0, owned, score_item, 0)
 
     def finish(step, carry):
         other = partner(step)
+        count_copy(other).wait_send()
         for item in range(owned):
             row_copy(other, item).wait_send()
             aux_copy(other, item).wait_send()
@@ -204,7 +241,6 @@
     rows, width = embeddings.shape
     average = rows // owned
     cap = 3 * rows // (2 * owned * n)
-    normed = unit_rows(embeddings)
     cover = jnp.concatenate(
         [coverage.reshape(1, rows), jnp.ones((1, rows), BF16), jnp.zeros((14, rows), BF16)], axis=0
     )
@@ -214,13 +250,17 @@
     gains, fresh = pl.pallas_call(
         functools.partial(kernel, n, owned, cap, average),
         out_shape=(
-            jax.ShapeDtypeStruct((owned, cands, 1), F32),
+            jax.ShapeDtypeStruct((owned, 1, cands), F32),
             jax.ShapeDtypeStruct((1, rows), F32),
         ),
-        in_specs=[vmem] * 4,
+        in_specs=[pl.BlockSpec(memory_space=pl.ANY)] + [vmem] * 3,
         out_specs=(vmem, vmem),
         scratch_shapes=[
+            pltpu.VMEM((rows, width), BF16),
             pltpu.VMEM((1, rows), jnp.int32),
+            pltpu.VMEM((n, owned, 128), F32),
+            pltpu.VMEM((n, owned, 128), F32),
+            pltpu.VMEM((owned, n + 1, 1, 128), F32),
             pltpu.VMEM((owned, n, cap, width), BF16),
             pltpu.VMEM((owned, n, cap, width), BF16),
             pltpu.VMEM((owned, n, 1, cap), F32),
@@ -231,11 +271,11 @@
             pltpu.VMEM((owned, n, 1, cap), F32),
             pltpu.VMEM((owned, n, 1, cap), F32),
             pltpu.VMEM((n * owned, cap), F32),
-        ] + [dma] * 6,
+        ] + [pltpu.SemaphoreType.DMA] + [pltpu.SemaphoreType.DMA((n,))] * 2 + [dma] * 6,
         compiler_params=pltpu.CompilerParams(
             collective_id=0, has_side_effects=True, vmem_limit_bytes=60 * 1024 * 1024
         ),
-    )(normed, cluster.reshape(1, rows), cover, raw)
+    )(embeddings, cluster.reshape(1, rows), cover, raw)
     return (gains.reshape(owned, cands), fresh.reshape(rows))
 
 

time: 270 us -> 240 us (0.89)
  Pallas kernels: 250 us -> 232 us
  other arithmetic: 15 us -> 1.44 us
    pallas_call x1, Pallas kernels: 250 us -> 232 us  [on_device(): pl.pallas_call(functools.partial(kernel, n, owned, cap, average), out_sha...]
    convert_element_type x1 -> x0, other arithmetic: 7.26 us -> none  [unit_rows(): return (widened * inverse).astype(BF16)]
    reduce_sum x1 -> x0, other arithmetic: 4.09 us -> none  [unit_rows(): jnp.sum(widened * widened, axis=1, keepdims=True) + 1e-06]
where the time goes in v2:
time: 240 us; the launch traced here: 239 us
  Pallas kernels  232 us (97%)
  local copies, waits for them, and re-layouts  4.85 us (2%)
    pallas_call x1, Pallas kernels, on_device(): pl.pallas_call(functools.partial(kernel, n, owned, cap, average), out_sha...  232 us

profile of v2, /device:TPU:0, one launch (start us, length us, event | category | flops | bytes accessed | tf_op | source)
XLA Modules:
  0.0 239.4 jit_solution(17727088137182894246)
XLA Ops:
  0.6 0.1 pad.1.clone
  0.7 0.1 pad.2.clone
  0.8 0.7 convert_bitcast_fusion
  1.5 0.7 reshape.20
  2.2 0.7 maximum_maximum_fusion.cover
  2.9 1.4 copy.6.raw
  4.3 232.4 %shard_map.59 = (f32[2,1,1024]{2,1,0:T(1,128)}, f32[1,4096]{1,0:T(1,128)}) custom-call(bf16[4096,768]{1,0:T(8,128)(2,1)} %embeddings.1, s32[1,4096]{1,0:T(1,128)} %bitcast.8, bf16[16,4096]{1,0:T(8,128)(2,1)} %maximum_maximum_fusion.cover, f32[2,1024,1]{2,1,0:T(8,128)} %copy.6.raw), custom_call_target="tpu_custom_call" | custom-call | tf_op jit(solution)/shard_map/pallas_call | solution.py:250
  236.8 1.3 copy.9
  238.1 1.3 copy.11
  (1 shorter events, 0.0 us)

commit v3 on v2

--- a/solution.py
+++ b/solution.py
@@ -23,6 +23,7 @@
     rows = held.shape[0]
     cands = raw.shape[1]
     clusters = n * owned
+    fold = relief_sum.shape[1] // cap
 
     load = pltpu.make_async_copy(embeddings, held, held_in)
     load.start()
@@ -181,15 +182,21 @@
         chosen[...] = chosen_sum[...].astype(BF16)
         relief_sum[...] = jnp.zeros_like(relief_sum)
 
-        def score_one(source, carry):
+        def score_one(part, carry):
+            first = part * fold
             scores = lax.dot_general(
-                chosen[...], got[item, source], (((1,), (1,)), ((), ())), preferred_element_type=F32
+                chosen[...],
+                got[item, pl.ds(first, fold)].reshape(fold * cap, chosen.shape[1]),
+                (((1,), (1,)), ((), ())), preferred_element_type=F32,
             )
-            relief_sum[...] += jnp.maximum(scores - got_aux[item, source], 0.0)
-            near_out[item, source] = jnp.max(scores, axis=0, keepdims=True)
+            aux = jnp.concatenate([got_aux[item, first + place] for place in range(fold)], axis=1)
+            relief_sum[...] += jnp.maximum(scores - aux, 0.0)
+            near = jnp.max(scores, axis=0, keepdims=True)
+            for place in range(fold):
+                near_out[item, first + place] = near[:, place * cap : (place + 1) * cap]
             return carry
 
-        lax.fori_loop(0, n, score_one, 0)
+        lax.fori_loop(0, n // fold, score_one, 0)
 
         def send_back(step, carry):
             near_copy(partner(step), item).start()
@@ -267,7 +274,7 @@
             pltpu.VMEM((owned, n, 1, cap), F32),
             pltpu.VMEM((cands, width), F32),
             pltpu.VMEM((cands, width), BF16),
-            pltpu.VMEM((cands, cap), F32),
+            pltpu.VMEM((cands, 4 * cap), F32),
             pltpu.VMEM((owned, n, 1, cap), F32),
             pltpu.VMEM((owned, n, 1, cap), F32),
             pltpu.VMEM((n * owned, cap), F32),

time: 240 us -> 236 us (0.983)
  Pallas kernels: 232 us -> 229 us
    pallas_call x1, Pallas kernels: 232 us -> 229 us  [on_device(): pl.pallas_call(functools.partial(kernel, n, owned, cap, average), out_sha...]
where the time goes in v3:
time: 236 us
  Pallas kernels  229 us (97%)
  local copies, waits for them, and re-layouts  4.85 us (2%)
    pallas_call x1, Pallas kernels, on_device(): pl.pallas_call(functools.partial(kernel, n, owned, cap, average), out_sha...  229 us

profile of v3, /device:TPU:0, one launch (start us, length us, event | category | flops | bytes accessed | tf_op | source)
XLA Modules:
  0.0 235.8 jit_solution(10710632941694960246)
XLA Ops:
  0.6 0.1 pad.1.clone
  0.7 0.1 pad.2.clone
  0.8 0.7 convert_bitcast_fusion
  1.5 0.7 reshape.20
  2.2 0.7 maximum_maximum_fusion.cover
  2.9 1.4 copy.6.raw
  4.3 228.8 %shard_map.59 = (f32[2,1,1024]{2,1,0:T(1,128)}, f32[1,4096]{1,0:T(1,128)}) custom-call(bf16[4096,768]{1,0:T(8,128)(2,1)} %embeddings.1, s32[1,4096]{1,0:T(1,128)} %bitcast.8, bf16[16,4096]{1,0:T(8,128)(2,1)} %maximum_maximum_fusion.cover, f32[2,1024,1]{2,1,0:T(8,128)} %copy.6.raw), custom_call_target="tpu_custom_call" | custom-call | tf_op jit(solution)/shard_map/pallas_call | solution.py:257
  233.1 1.3 copy.9
  234.4 1.3 copy.11
  (1 shorter events, 0.0 us)

commit v4 on v3

--- a/solution.py
+++ b/solution.py
@@ -193,18 +193,21 @@
             relief_sum[...] += jnp.maximum(scores - aux, 0.0)
             near = jnp.max(scores, axis=0, keepdims=True)
             for place in range(fold):
-                near_out[item, first + place] = near[:, place * cap : (place + 1) * cap]
+                source = first + place
+                near_out[item, source] = near[:, place * cap : (place + 1) * cap]
+
+                @pl.when(source != me)
+                def _():
+                    near_copy(source, item).start()
+
             return carry
 
         lax.fori_loop(0, n // fold, score_one, 0)
 
-        def send_back(step, carry):
-            near_copy(partner(step), item).start()
-            return carry
-
-        lax.fori_loop(0, n - 1, send_back, 0)
         near_in[item, me] = near_out[item, me]
-        gains[item] = jnp.sum(relief_sum[...].T, axis=0, keepdims=True) / average
+        lanes = 128 if fold * cap % 128 == 0 else fold * cap
+        folded = sum(relief_sum[:, at : at + lanes] for at in range(0, fold * cap, lanes))
+        gains[item] = jnp.sum(folded.T, axis=0, keepdims=True) / average
         return carry
 
     lax.fori_loop(0, owned, score_item, 0)

time: 236 us -> 234 us (level)
  Pallas kernels: 229 us -> 226 us
    pallas_call x1, Pallas kernels: 229 us -> 226 us  [on_device(): pl.pallas_call(functools.partial(kernel, n, owned, cap, average), out_sha...]
where the time goes in v4:
time: 234 us; the launch traced here: 233 us
  Pallas kernels  226 us (97%)
  local copies, waits for them, and re-layouts  4.85 us (2%)
    pallas_call x1, Pallas kernels, on_device(): pl.pallas_call(functools.partial(kernel, n, owned, cap, average), out_sha...  226 us

profile of v4, /device:TPU:0, one launch (start us, length us, event | category | flops | bytes accessed | tf_op | source)
XLA Modules:
  0.0 232.7 jit_solution(10522917322959998132)
XLA Ops:
  0.6 0.1 pad.1.clone
  0.7 0.1 pad.2.clone
  0.8 0.7 convert_bitcast_fusion
  1.5 0.7 reshape.20
  2.2 0.7 maximum_maximum_fusion.cover
  2.9 1.4 copy.6.raw
  4.3 225.8 %shard_map.59 = (f32[2,1,1024]{2,1,0:T(1,128)}, f32[1,4096]{1,0:T(1,128)}) custom-call(bf16[4096,768]{1,0:T(8,128)(2,1)} %embeddings.1, s32[1,4096]{1,0:T(1,128)} %bitcast.8, bf16[16,4096]{1,0:T(8,128)(2,1)} %maximum_maximum_fusion.cover, f32[2,1024,1]{2,1,0:T(8,128)} %copy.6.raw), custom_call_target="tpu_custom_call" | custom-call | tf_op jit(solution)/shard_map/pallas_call | solution.py:260
  230.1 1.3 copy.9
  231.4 1.3 copy.11
  (1 shorter events, 0.0 us)
